TPU v7x, 32 devices: a whole 2x2x4 slice. The times are simulated.
32 devices in a mesh: group: 2 (over y), scen: 4 (over z), site: 4 (over x, core).
Axes of the slice: x: 2, y: 2, z: 4, core: 2. Of those that a mesh axis runs over, the one named last changes fastest.
Arguments:
- dispatch: float32 [128, 256, 256], P(('group', 'scen'), 'site'), parts along dimension 0, may hold values from -6 to 6
- dual_price: float32 [128, 256, 256], P(('group', 'scen'), 'site'), parts along dimension 0, may hold values from -4 to 4
- net_load: bfloat16 [128, 256, 256], P(('group', 'scen'), 'site'), parts along dimension 0, may hold values from -6 to 6
- energy_price: float32 [512, 256], P(('group', 'site')), parts along dimension 0, may hold values from -4 to 4
- penalty: float32 [256], P('site'), may hold values from 0.5 to 2
- soc_weight: float32 [256], P('site'), may hold values from 2 to 20
- capacity: float32 [256], P('site'), may hold values from 1 to 3
- probability: float32 [128], P('group'), parts along dimension 0, may hold values from 0.3 to 9, as said below
- node_deep: int32 [128], P('group'), parts along dimension 0, may hold values from 0 to 7, never falling along the last dimension, each value on 1 to 16 neighbouring positions
Outputs:
- new_dispatch: float32 [128, 256, 256], P(('group', 'scen'), 'site'), parts along dimension 0
- new_dual: float32 [128, 256, 256], P(('group', 'scen'), 'site'), parts along dimension 0
There are 2 independent parts, one for each index of `group`. A program takes and returns all parts, laid end to end along the dimension named above; an argument that names none is the same for every part. Nothing has to cross between parts.
Inputs may be any that keep to these rules, and one draw needn't show every extreme that they name: `probability`: scenario weights are positive. node_deep never falls along the scenarios; each node holds 1 to 16 scenarios, one exactly 16.
All inputs are finite; a program needn't handle non-finite values.
Results may differ from a plain program's by a relative error of at most 0.0003.
Values sent between devices are 32-bit elements; how exact they have to be, the bound alone decides.
A program may use at most 64 MiB of HBM per device.

v0:
```python
import jax
import jax.numpy as jnp
from jax import lax
from jax.sharding import PartitionSpec as P

DEEP = 8
BRANCH = 4


precise = lax.Precision.HIGHEST


def triangle(horizon):
    row_ids = lax.broadcasted_iota(jnp.int32, (horizon, horizon), 0)
    col_ids = lax.broadcasted_iota(jnp.int32, (horizon, horizon), 1)
    return (row_ids <= col_ids).astype(jnp.float32)


def node_totals(all_ids, weights, node_count):
    indicator = (all_ids[None, :] == jnp.arange(node_count, dtype=jnp.int32)[:, None]).astype(
        jnp.float32
    )
    return jnp.dot(indicator, weights, precision=precise)


def lookup_totals(my_ids, totals):
    indicator = (my_ids[:, None] == jnp.arange(totals.shape[0], dtype=jnp.int32)[None, :]).astype(
        jnp.float32
    )
    return jnp.dot(indicator, totals, precision=precise)


def level_table(my_ids, weighted, node_count):
    indicator = (my_ids[None, :] == jnp.arange(node_count, dtype=jnp.int32)[:, None]).astype(
        jnp.float32
    )
    return (indicator, jnp.dot(indicator, weighted, precision=precise))


def body(
    dispatch,
    dual_price,
    net_load,
    energy_price,
    penalty,
    soc_weight,
    capacity,
    probability,
    node_deep,
):
    scen_count, site_count, horizon = dispatch.shape
    section_hours = horizon // 4
    width = site_count * section_hours
    first_row = lax.axis_index("scen") * scen_count
    my_prob = lax.dynamic_slice_in_dim(probability, first_row, scen_count)
    my_deep = lax.dynamic_slice_in_dim(node_deep, first_row, scen_count)
    my_upper = my_deep // BRANCH
    deep_count = node_deep.shape[0] // DEEP
    upper_count = deep_count // BRANCH

    def weighted_section(section_index):
        piece = dispatch[:, :, section_index * section_hours : (section_index + 1) * section_hours]
        return (my_prob[:, None, None] * piece).reshape(scen_count, width)

    root_part = jnp.sum(weighted_section(0), axis=0)
    upper_part = weighted_section(1)
    deep_part = weighted_section(2)
    upper_pick, upper_table = level_table(my_upper, upper_part, upper_count)
    deep_pick, deep_table = level_table(my_deep, deep_part, deep_count)
    root_sum, upper_table, deep_table = lax.psum((root_part, upper_table, deep_table), "scen")
    upper_sums = jnp.dot(upper_pick.T, upper_table, precision=precise)
    deep_sums = jnp.dot(deep_pick.T, deep_table, precision=precise)
    upper_den = lookup_totals(my_upper, node_totals(node_deep // BRANCH, probability, upper_count))
    deep_den = lookup_totals(my_deep, node_totals(node_deep, probability, deep_count))
    root_mean = (root_sum / jnp.sum(probability)).reshape(site_count, section_hours)
    section_shape = (scen_count, site_count, section_hours)
    node_mean = jnp.concatenate(
        [
            jnp.broadcast_to(root_mean[None], section_shape),
            (upper_sums / upper_den[:, None]).reshape(section_shape),
            (deep_sums / deep_den[:, None]).reshape(section_shape),
            dispatch[:, :, 3 * section_hours :],
        ],
        axis=2,
    )
    penalty_rate = penalty[None, :, None]
    new_dual = dual_price + penalty_rate * (dispatch - node_mean)
    step_size = 0.5 / (1.0 + penalty_rate)
    limit = capacity[None, :, None]
    charge_scale = soc_weight[None, :, None] / (horizon * horizon)
    sites_all = site_count * lax.axis_size("site")
    load_float = net_load.astype(jnp.float32)
    upper_ones = triangle(horizon)
    current = dispatch
    for sweep_index in range(2):
        flat = current.reshape(scen_count * site_count, horizon)
        charge_state = jnp.dot(flat, upper_ones, precision=precise)
        ahead = jnp.dot(charge_state, upper_ones.T, precision=precise).reshape(current.shape)
        imbalance = lax.psum(jnp.sum(current - load_float, axis=1), "site")
        gradient = (
            energy_price[None]
            + new_dual
            + penalty_rate * (current - node_mean)
            + charge_scale * ahead
            + 2.0 / sites_all * imbalance[:, None, :]
        )
        current = jnp.clip(current - step_size * gradient, -limit, limit)
    return (current, new_dual)


def solution(mesh):
    in_specs = (
        P(("group", "scen"), "site", None),
        P(("group", "scen"), "site", None),
        P(("group", "scen"), "site", None),
        P(("group", "site"), None),
        P("site"),
        P("site"),
        P("site"),
        P("group"),
        P("group"),
    )
    out_specs = (P(("group", "scen"), "site", None), P(("group", "scen"), "site", None))
    return jax.shard_map(body, mesh=mesh, in_specs=in_specs, out_specs=out_specs, check_vma=False)
```

profile of v0, /device:TPU:0, one launch (start us, length us, event | category | flops | bytes accessed | tf_op | source)
XLA Modules:
  0.0 79.2 jit_solution(4776916023686924647)
XLA Ops:
  7.2 0.0 all-reduce.3.cloned.1.call-start
  7.2 0.0 copy-start.12
  7.2 0.6 copy-done.12
  7.9 0.0 copy-start.11
  7.9 0.1 dynamic_slice.6
  7.9 0.6 copy-done.11
  8.5 0.1 and_select_fusion.1
  8.6 0.0 copy-start.6
  8.6 2.7 %multiply_reduce_fusion = (f32[64,64]{1,0:T(8,128)S(1)}, f32[16,64,64]{2,1,0:T(8,128)S(1)}, f32[16,64,64]{2,1,0:T(8,128)S(1)}, f32[16,64,64]{2,1,0:T(8,128)}) fusion(f32[16,64,256]{2,1,0:T(8,128)} %param.9, f32[16]{0:T(128)S(1)} %dynamic_slice.6), kind=kLoop, calls=%fused_computation.17 | loop fusion | flops 258048 | bytes 1851456 | tf_op jit(solution)/shard_map/reduce_sum | solution.py:65
  11.3 0.0 copy-start
  11.3 0.2 reshape.56
  11.5 0.9 %fusion.10 = f32[8,4096]{1,0:T(8,128)} fusion(f32[16,4096]{1,0:T(8,128)S(1)} %reshape.56, s32[16]{0:T(128)S(1)} %get-tuple-element.8), kind=kOutput, calls=%fused_computation.32 | convolution fusion | flops 6291584 | bytes 393280 | tf_op jit(solution)/shard_map/dot_general | solution.py:37
  12.4 0.0 all-reduce.3.cloned.1.call-update
  12.4 0.6 reduce_sum.40
  13.0 0.1 convolution_bitcast_fusion
  13.2 0.0 copy-done.6
  13.2 0.0 copy-done
  13.2 0.2 fusion
  13.4 13.1 %psum.38 = f32[16,256]{1,0:T(8,128)S(1)} all-reduce(f32[16,256]{1,0:T(8,128)S(1)} %fusion), channel_id=1, replica_groups=mesh['group'=2,'scen'=4,'site'=4] {'site'}, use_global_device_ids=true, to_apply=%region_6.7 | all-reduce | flops 4096 | bytes 32768 | tf_op jit(solution)/shard_map/psum | solution.py:99
  26.4 0.7 fusion.7
  27.1 2.0 %fusion.5 = f32[1024,256]{1,0:T(8,128)} fusion(f32[256,1024]{1,0:T(8,128)S(1)} %fusion.7), kind=kOutput, calls=%fused_computation.21 | convolution fusion | flops 805371904 | bytes 2097152 | tf_op jit(solution)/shard_map/dot_general | solution.py:98
  29.1 0.1 reduce_sum.39
  29.2 0.2 reshape.54
  29.4 0.2 convolution_bitcast_fusion.2
  29.6 0.0 copy-start.8
  29.6 0.0 copy-start.10
  29.6 0.2 fusion.17
  29.8 0.4 copy-done.8
  30.2 0.0 copy-done.10
  30.3 19.5 %all-reduce = (f32[2,4096]{1,0:T(2,128)S(1)}, f32[4096]{0:T(1024)S(1)}) all-reduce(f32[2,4096]{1,0:T(2,128)S(1)} %fusion.17, f32[4096]{0:T(1024)S(1)} %reduce_sum.39), channel_id=1, replica_groups=mesh['group'=2,'scen'=4,'site'=4] {'scen'}, use_global_device_ids=true, to_apply=%region_3.4 | all-reduce | flops 12288 | bytes 98304 | tf_op jit(solution)/shard_map/psum | solution.py:70
  49.8 0.6 broadcast_divide_fusion
  50.4 0.4 convolution_divide_fusion.1
  50.8 0.0 copy-start.9
  50.8 0.1 convolution_bitcast_fusion.3
  50.9 0.5 copy-done.9
  51.4 0.1 broadcast_in_dim.4
  51.5 0.2 reshape.55
  51.7 0.2 convolution_bitcast_fusion.1
  51.9 0.0 all-reduce.3.cloned.1.call-done
  51.9 1.2 %convolution_divide_fusion = f32[16,4096]{1,0:T(8,128)S(1)} fusion(f32[8,4096]{1,0:T(8,128)} %all-reduce.3.cloned.1.call-done, f32[16]{0:T(128)S(1)} %convolution_bitcast_fusion.1, s32[16]{0:T(128)S(1)} %get-tuple-element.8), kind=kOutput, calls=%fused_computation | convolution fusion | flops 6357120 | bytes 393344 | tf_op jit(solution)/shard_map/dot_general | solution.py:72
  53.2 0.0 copy-start.7
  53.2 0.2 reshape.57
  53.4 0.0 copy-start.3
  53.5 0.5 copy-done.7
  54.0 0.4 copy-done.3
  54.4 0.0 copy-start.1
  54.5 3.8 %fusion.1 = (f32[16,256]{1,0:T(8,128)S(1)}, f32[16,64,256]{2,1,0:T(8,128)S(1)}, f32[16,64,256]{2,1,0:T(8,128)}) fusion(bf16[16,64,256]{2,1,0:T(8,128)(2,1)} %param.11, f32[16,64,256]{2,1,0:T(8,128)S(1)} %copy-done, f32[16,256]{1,0:T(8,128)S(1)} %broadcast_multiply_fusion.1, f32[64]{0:T(128)S(1)} %get-tuple-element.14, f32[16,64,64]{2,1,0:T(8,128)S(1)} %copy-done.3, ...), kind=kLoop, calls=%fused_computation.9 | loop fusion | flops 4714496 | bytes 6915328 | tf_op jit(solution)/shard_map/reduce_sum | solution.py:99
  58.3 0.0 copy-done.1
  58.3 10.2 %psum.39 = f32[16,256]{1,0:T(8,128)S(1)} all-reduce(f32[16,256]{1,0:T(8,128)S(1)} %get-tuple-element.4), channel_id=1, replica_groups=mesh['group'=2,'scen'=4,'site'=4] {'site'}, use_global_device_ids=true, to_apply=%region_8.9 | all-reduce | flops 4096 | bytes 32768 | tf_op jit(solution)/shard_map/psum | solution.py:99
  68.4 0.6 fusion.4
  69.1 0.0 copy-start.2
  69.1 0.0 copy-start.4
  69.1 0.0 copy-start.5
  69.1 0.6 fusion.3
  69.7 0.4 copy-done.2
  70.1 0.2 copy-done.4
  70.3 0.3 copy-done.5
  70.6 1.8 %maximum_minimum_fusion = f32[16,64,256]{2,1,0:T(8,128)} fusion(f32[16,64,256]{2,1,0:T(8,128)S(1)} %get-tuple-element.5, f32[16,64,256]{2,1,0:T(8,128)S(1)} %bitcast.33, f32[16,64,256]{2,1,0:T(8,128)S(1)} %copy-done.5, f32[16,256]{1,0:T(8,128)S(1)} %broadcast_multiply_fusion, f32[64]{0:T(128)S(1)} %get-tuple-element.14, f32[64]{0:T(128)S(1)} %copy-done.8, ...), kind=kLoop, calls=%fused_computation.11 | loop fusion | flops 3670016 | bytes 5326080 | tf_op jit(solution)/shard_map/jit(clip)/min | solution.py:107
  (6 shorter events, 0.1 us)
Async XLA Ops:
  7.2 44.8 %all-reduce.3.cloned.1.call-start = ((), (), s32[]{:S(2)}) async-start(), calls=%async_computation | async-start | bytes 262144 | tf_op jit(solution)/shard_map/psum | solution.py:70
  7.2 0.7 copy-start.12
  7.9 0.7 copy-start.11
  8.6 4.6 %copy-start.6 = (bf16[16,64,256]{2,1,0:T(8,128)(2,1)S(1)}, bf16[16,64,256]{2,1,0:T(8,128)(2,1)}, u32[]{:S(2)}) copy-start(bf16[16,64,256]{2,1,0:T(8,128)(2,1)} %param.11) | copy-start | bytes 1572868
  11.3 1.8 %copy-start = (f32[16,64,256]{2,1,0:T(8,128)S(1)}, f32[16,64,256]{2,1,0:T(8,128)}, u32[]{:S(2)}) copy-start(f32[16,64,256]{2,1,0:T(8,128)} %param.9) | copy-start | bytes 3145732
  29.6 0.7 copy-start.8
  29.6 0.7 copy-start.10
  50.8 0.7 copy-start.9
  53.2 0.8 %copy-start.7 = (f32[64,256]{1,0:T(8,128)S(1)}, f32[64,256]{1,0:T(8,128)}, u32[]{:S(2)}) copy-start(f32[64,256]{1,0:T(8,128)} %param.12) | copy-start | bytes 196612
  53.4 1.1 %copy-start.3 = (f32[16,64,64]{2,1,0:T(8,128)S(1)}, f32[16,64,64]{2,1,0:T(8,128)}, u32[]{:S(2)}) copy-start(f32[16,64,64]{2,1,0:T(8,128)} %get-tuple-element.12) | copy-start | bytes 786436
  54.4 3.8 %copy-start.1 = (f32[16,64,64]{2,1,0:T(8,128)}, f32[16,64,64]{2,1,0:T(8,128)S(1)}, u32[]{:S(2)}) copy-start(f32[16,64,64]{2,1,0:T(8,128)S(1)} %broadcast_in_dim.5) | copy-start | bytes 786436
  69.1 1.0 %copy-start.2 = (f32[16,64,64]{2,1,0:T(8,128)S(1)}, f32[16,64,64]{2,1,0:T(8,128)}, u32[]{:S(2)}) copy-start(f32[16,64,64]{2,1,0:T(8,128)} %copy-done.1) | copy-start | bytes 786436
  69.1 1.2 %copy-start.4 = (f32[16,64,64]{2,1,0:T(8,128)S(1)}, f32[16,64,64]{2,1,0:T(8,128)}, u32[]{:S(2)}) copy-start(f32[16,64,64]{2,1,0:T(8,128)} %get-tuple-element.12) | copy-start | bytes 786436
  69.1 1.5 %copy-start.5 = (f32[16,64,256]{2,1,0:T(8,128)S(1)}, f32[16,64,256]{2,1,0:T(8,128)}, u32[]{:S(2)}) copy-start(f32[16,64,256]{2,1,0:T(8,128)} %get-tuple-element.6) | copy-start | bytes 3145732
Sparse Core Ops, SparseCore 0:
  12.5 37.1 all-reduce.2
where the time goes:
time: 79.6 us; the launch traced here: 79.2 us
  blocking collectives  42.7 us (54%)
  between operations  14.2 us (18%)
  other arithmetic  9.82 us (12%)
  matrix products  7.24 us (9%)
  local copies, waits for them, and re-layouts  5.17 us (6%)
    psum x2, blocking collectives, body(): imbalance = lax.psum(jnp.sum(current - load_float, axis=1), 'site')  23.2 us
    psum x1, blocking collectives, body(): lax.psum((root_part, upper_table, deep_table), 'scen')  19.5 us
    unnamed x26, local copies, waits for them, and re-layouts  4.11 us
    reduce_sum x2, other arithmetic, body(): imbalance = lax.psum(jnp.sum(current - load_float, axis=1), 'site')  3.99 us
    reduce_sum x1, other arithmetic, body(): root_part = jnp.sum(weighted_section(0), axis=0)  2.73 us
    dot_general x2, matrix products, body(): jnp.dot(charge_state, upper_ones.T, precision=precise)  2.62 us
    min x1, other arithmetic, body(): current = jnp.clip(current - step_size * gradient, -limit, limit)  1.75 us
  transfers between devices with their start and end apart: 1, of which 0 were waited for; matrix products, arithmetic and copies ran while one was open for 7% of the time, Pallas kernels for 0%

commit v1 on v0

v1 whole, which is shorter than its diff:
```python
import functools

import jax
import jax.numpy as jnp
from jax import lax
from jax.experimental import pallas as pl
from jax.experimental.pallas import tpu as pltpu
from jax.sharding import PartitionSpec as P

BRANCH = 4
MESH = pl.DeviceIdType.MESH
CHUNKS = 4


def kernel(
    n_scen,
    n_site,
    disp_hbm,
    dual_hbm,
    load_hbm,
    energy_hbm,
    pen_ref,
    soc_ref,
    cap_ref,
    prob_ref,
    node_ref,
    out_hbm,
    ndual_hbm,
    x_ref,
    dual_ref,
    load_ref,
    energy_ref,
    floc_ref,
    q_ref,
    z_ref,
    cur_ref,
    nd_ref,
    fin_ref,
    kern_ref,
    tab_ref,
    col_ref,
    pay_ref,
    payd_ref,
    got_ref,
    gotd_ref,
    imb_ref,
    imbr_ref,
    loadsum_ref,
    in_sem,
    out_sem,
    scen_send,
    scen_recv,
    deep_send,
    deep_recv,
    site_send,
    site_recv,
):
    scen_count, site_count, horizon = x_ref.shape
    hours = horizon // 4
    half = horizon // 2
    step_rows = scen_count // CHUNKS
    me = lax.axis_index("scen")
    here = lax.axis_index("site")

    def rows(c):
        return pl.ds(c * step_rows, step_rows)

    def fetch(c, which, src, dst):
        return pltpu.make_async_copy(src.at[rows(c)], dst.at[rows(c)], in_sem.at[which, c])

    ins = []
    for c in range(CHUNKS):
        ins.append((fetch(c, 0, disp_hbm, x_ref), fetch(c, 1, load_hbm, load_ref)))
        ins[c][0].start()
        ins[c][1].start()
    energy_in = pltpu.make_async_copy(energy_hbm, energy_ref, in_sem.at[3, 0])
    energy_in.start()
    dual_in = [fetch(c, 2, dual_hbm, dual_ref) for c in range(CHUNKS)]
    for c in range(CHUNKS):
        dual_in[c].start()

    @pl.when(me == 0)
    def _():
        gotd_ref[0] = jnp.zeros_like(gotd_ref[0])

    @pl.when(me == n_scen - 1)
    def _():
        gotd_ref[1] = jnp.zeros_like(gotd_ref[1])

    barrier = pltpu.get_barrier_semaphore()
    for j in range(1, n_scen):
        pl.semaphore_signal(
            barrier, inc=1, device_id={"scen": lax.rem(me + j, n_scen)}, device_id_type=MESH
        )
    for j in range(1, n_site):
        pl.semaphore_signal(
            barrier, inc=1, device_id={"site": lax.rem(here + j, n_site)}, device_id_type=MESH
        )

    total = prob_ref.shape[0]
    first_row = me * scen_count
    prob = prob_ref[...].reshape(1, total)
    node_int = node_ref[...].reshape(1, total)
    deep = node_int.astype(jnp.float32)
    upper = lax.div(node_int, jnp.full_like(node_int, BRANCH)).astype(jnp.float32)
    lane = lax.broadcasted_iota(jnp.int32, (scen_count, total), 1)
    sub = lax.broadcasted_iota(jnp.int32, (scen_count, total), 0)
    lane1 = lax.broadcasted_iota(jnp.int32, (1, total), 1)

    def pick(mask, row):
        return jnp.sum(jnp.where(mask, row, 0.0), axis=1, keepdims=True)

    own = lane == sub + first_row
    before = lane == sub + (first_row - 1)
    my_prob, my_deep, my_upper = pick(own, prob), pick(own, deep), pick(own, upper)
    first = lane1 == first_row
    last = lane1 == first_row + (scen_count - 1)
    first_deep, first_upper = pick(first, deep), pick(first, upper)
    last_deep, last_upper = pick(last, deep), pick(last, upper)

    def same(a, b):
        return jnp.where(a == b, 1.0, 0.0)

    section = lax.broadcasted_iota(jnp.int32, (scen_count, horizon), 1)

    def table(root, up, dp, leaf):
        return jnp.where(
            section < hours,
            root,
            jnp.where(section < 2 * hours, up, jnp.where(section < 3 * hours, dp, leaf)),
        )

    inv_root = 1.0 / jnp.sum(prob, axis=1, keepdims=True)
    inv_upper = 1.0 / pick(my_upper == upper, prob)
    inv_deep = 1.0 / pick(my_deep == deep, prob)
    inv = table(inv_root, inv_upper, inv_deep, 1.0)
    from_left = table(1.0, same(my_upper, first_upper), same(my_deep, first_deep), 0.0)
    from_right = table(1.0, same(my_upper, last_upper), same(my_deep, last_deep), 0.0)
    tab_ref[0] = table(my_prob, my_prob, my_prob, 1.0)
    tab_ref[1] = table(
        1.0, same(my_upper, pick(before, upper)), same(my_deep, pick(before, deep)), 0.0
    )
    tab_ref[2] = from_left
    tab_ref[3] = inv
    tab_ref[4] = inv * from_left
    tab_ref[5] = inv * from_right

    eye = lax.broadcasted_iota(jnp.int32, (site_count, site_count), 0) == (
        lax.broadcasted_iota(jnp.int32, (site_count, site_count), 1)
    )

    def column(ref):
        return pick(eye, ref[...].reshape(1, site_count))

    pen = column(pen_ref)
    step = 0.5 / (1.0 + pen)
    wide = (site_count, horizon)
    sites_all = site_count * n_site
    col_ref[0] = jnp.broadcast_to(pen, wide)
    col_ref[1] = jnp.broadcast_to(step, wide)
    col_ref[2] = jnp.broadcast_to(step * column(soc_ref) / (horizon * horizon), wide)
    col_ref[3] = jnp.broadcast_to(step * (2.0 / sites_all), wide)
    col_ref[4] = jnp.broadcast_to(column(cap_ref), wide)
    hour_a = lax.broadcasted_iota(jnp.int32, (horizon, horizon), 0)
    hour_b = lax.broadcasted_iota(jnp.int32, (horizon, horizon), 1)
    kern_ref[...] = (horizon - jnp.maximum(hour_a, hour_b)).astype(jnp.float32).astype(kern_ref.dtype)

    def ahead_of(ref, c):
        flat = ref[rows(c)].reshape(step_rows * site_count, horizon)
        if kern_ref.dtype == jnp.bfloat16:
            high = flat.astype(jnp.bfloat16)
            low = (flat - high.astype(jnp.float32)).astype(jnp.bfloat16)
            ahead = jnp.dot(high, kern_ref[...], preferred_element_type=jnp.float32) + jnp.dot(
                low, kern_ref[...], preferred_element_type=jnp.float32
            )
        else:
            ahead = jnp.dot(flat, kern_ref[...], precision=lax.Precision.HIGHEST)
        return ahead.reshape(step_rows, site_count, horizon)

    def row(ref, s):
        return ref[pl.ds(s, 1), :]

    fore = None
    first_sum = None
    for c in range(CHUNKS):
        ins[c][0].wait()
        ins[c][1].wait()
        for s in range(c * step_rows, (c + 1) * step_rows):
            x = x_ref[s]
            load_total = jnp.sum(load_ref[s].astype(jnp.float32), axis=0, keepdims=True)
            loadsum_ref[pl.ds(s, 1), :] = load_total
            imb_ref[0, pl.ds(s, 1), :] = jnp.sum(x, axis=0, keepdims=True) - load_total
            weighted = x * row(tab_ref.at[0], s)
            fore = weighted if fore is None else weighted + row(tab_ref.at[1], s) * fore
            floc_ref[s] = fore
            part = weighted * row(tab_ref.at[2], s)
            first_sum = part if first_sum is None else first_sum + part

    half_lane = lax.broadcasted_iota(jnp.int32, (site_count // 2, half), 1)

    def fill(slot, value):
        pay_ref[slot] = value[:, :half]
        tail = value[:, half:]
        payd_ref[slot] = jnp.where(
            half_lane < hours,
            tail[: site_count // 2],
            pltpu.roll(tail[site_count // 2 :], hours, axis=1),
        )

    fill(0, fore)
    fill(1, first_sum)

    pl.semaphore_wait(barrier, n_scen + n_site - 2)

    scen_copies = []
    for j in range(1, n_scen):
        peer = lax.rem(me + j, n_scen)
        side = jnp.where(peer > me, 0, 1)
        scen_copies.append(
            pltpu.make_async_remote_copy(
                src_ref=pay_ref.at[side],
                dst_ref=got_ref.at[j - 1],
                send_sem=scen_send.at[j - 1],
                recv_sem=scen_recv.at[j - 1],
                device_id={"scen": peer},
                device_id_type=MESH,
            )
        )
    deep_copies = []
    for side, peer in ((0, jnp.minimum(me + 1, n_scen - 1)), (1, jnp.maximum(me - 1, 0))):
        deep_copies.append(
            pltpu.make_async_remote_copy(
                src_ref=payd_ref.at[side],
                dst_ref=gotd_ref.at[side],
                send_sem=deep_send.at[side],
                recv_sem=deep_recv.at[side],
                device_id={"scen": peer},
                device_id_type=MESH,
            )
        )
    has_right = me < n_scen - 1
    has_left = me > 0

    def site_copies(turn):
        return [
            pltpu.make_async_remote_copy(
                src_ref=imb_ref.at[turn],
                dst_ref=imbr_ref.at[turn, j - 1],
                send_sem=site_send.at[turn, j - 1],
                recv_sem=site_recv.at[turn, j - 1],
                device_id={"site": lax.rem(here + j, n_site)},
                device_id_type=MESH,
            )
            for j in range(1, n_site)
        ]

    for copy in scen_copies:
        copy.start()

    @pl.when(has_right)
    def _():
        deep_copies[0].start()

    @pl.when(has_left)
    def _():
        deep_copies[1].start()

    sites_first = site_copies(0)
    for copy in sites_first:
        copy.start()

    energy_in.wait()
    fin_ref[0] = col_ref[1] * energy_ref[...]
    back = None
    for s in reversed(range(scen_count)):
        if back is None:
            back = floc_ref[s]
        else:
            back = jnp.where(row(tab_ref.at[1], s + 1) > 0.5, back, floc_ref[s])
        q_ref[s] = col_ref[0] * (x_ref[s] - back * row(tab_ref.at[3], s))
    for c in range(CHUNKS):
        ahead = ahead_of(x_ref, c)
        dual_in[c].wait()
        for i in range(step_rows):
            s = c * step_rows + i
            z_ref[s] = x_ref[s] - fin_ref[0] - col_ref[1] * dual_ref[s] - col_ref[2] * ahead[i]

    left = jnp.zeros((site_count, half), jnp.float32)
    right = jnp.zeros((site_count, half), jnp.float32)
    front_lane = lax.broadcasted_iota(jnp.int32, (1, half), 1)
    gates = []
    for j in range(1, n_scen):
        peer = lax.rem(me + (n_scen - j), n_scen)
        peer_last = lane1 == peer * scen_count + (scen_count - 1)
        peer_first = lane1 == peer * scen_count
        is_left = jnp.where(peer < me, 1.0, 0.0)
        gates.append(
            (
                is_left * jnp.where(front_lane < hours, 1.0, same(pick(peer_last, upper), first_upper)),
                (1.0 - is_left)
                * jnp.where(front_lane < hours, 1.0, same(pick(peer_first, upper), last_upper)),
            )
        )
    gate_left = same(pick(lane1 == first_row - 1, deep), first_deep)
    gate_right = same(pick(lane1 == first_row + scen_count, deep), last_deep)

    def unpack(value):
        return jnp.concatenate([value, pltpu.roll(value, hours, axis=1)], axis=0)

    for copy in sites_first:
        copy.wait_recv()
    imb_one = imb_ref[0]
    for j in range(n_site - 1):
        imb_one = imb_one + imbr_ref[0, j]
    tab_ref[0] = imb_one

    @pl.when(has_left)
    def _():
        deep_copies[0].wait_recv()

    @pl.when(has_right)
    def _():
        deep_copies[1].wait_recv()

    for j in range(1, n_scen):
        scen_copies[j - 1].wait_recv()
        got = got_ref[j - 1]
        left = left + gates[j - 1][0] * got
        right = right + gates[j - 1][1] * got
    fin_ref[1] = col_ref[0] * jnp.concatenate([left, gate_left * unpack(gotd_ref[0])], axis=1)
    fin_ref[2] = col_ref[0] * jnp.concatenate([right, gate_right * unpack(gotd_ref[1])], axis=1)

    for s in range(scen_count):
        q = (
            q_ref[s]
            - row(tab_ref.at[4], s) * fin_ref[1]
            - row(tab_ref.at[5], s) * fin_ref[2]
        )
        nd_ref[s] = dual_ref[s] + q
        cap = col_ref[4]
        new = z_ref[s] - 2.0 * col_ref[1] * q - col_ref[3] * row(tab_ref.at[0], s)
        new = jnp.minimum(jnp.maximum(new, -cap), cap)
        cur_ref[s] = new
        imb_ref[1, pl.ds(s, 1), :] = jnp.sum(new, axis=0, keepdims=True) - row(loadsum_ref, s)

    sites_second = site_copies(1)
    for copy in sites_second:
        copy.start()
    dual_out = pltpu.make_async_copy(nd_ref, ndual_hbm, out_sem.at[0])
    dual_out.start()

    for c in range(CHUNKS):
        ahead = ahead_of(cur_ref, c)
        for i in range(step_rows):
            s = c * step_rows + i
            now = cur_ref[s]
            z_ref[s] = (
                now
                - fin_ref[0]
                - col_ref[1]
                * (2.0 * nd_ref[s] - dual_ref[s] + col_ref[0] * (now - x_ref[s]))
                - col_ref[2] * ahead[i]
            )

    for copy in sites_second:
        copy.wait_recv()
    imb_two = imb_ref[1]
    for j in range(n_site - 1):
        imb_two = imb_two + imbr_ref[1, j]
    tab_ref[1] = imb_two
    outs = []
    for c in range(CHUNKS):
        for i in range(step_rows):
            s = c * step_rows + i
            cap = col_ref[4]
            new = z_ref[s] - col_ref[3] * row(tab_ref.at[1], s)
            q_ref[s] = jnp.minimum(jnp.maximum(new, -cap), cap)
        copy = pltpu.make_async_copy(q_ref.at[rows(c)], out_hbm.at[rows(c)], out_sem.at[c + 1])
        copy.start()
        outs.append(copy)

    for copy in scen_copies + sites_first + sites_second:
        copy.wait_send()

    @pl.when(has_right)
    def _():
        deep_copies[0].wait_send()

    @pl.when(has_left)
    def _():
        deep_copies[1].wait_send()

    dual_out.wait()
    for copy in outs:
        copy.wait()


def body(
    n_scen,
    n_site,
    dispatch,
    dual_price,
    net_load,
    energy_price,
    penalty,
    soc_weight,
    capacity,
    probability,
    node_deep,
):
    scen_count, site_count, horizon = dispatch.shape
    f32 = jnp.float32
    full = (scen_count, site_count, horizon)
    half = horizon // 2
    vmem = pltpu.VMEM
    any_spec = pl.BlockSpec(memory_space=pl.ANY)
    vmem_spec = pl.BlockSpec(memory_space=vmem)
    kern_type = jnp.bfloat16 if horizon <= 256 else f32
    dma = pltpu.SemaphoreType.DMA
    return pl.pallas_call(
        functools.partial(kernel, n_scen, n_site),
        out_shape=(jax.ShapeDtypeStruct(full, f32), jax.ShapeDtypeStruct(full, f32)),
        in_specs=[any_spec] * 4 + [vmem_spec] * 5,
        out_specs=(any_spec, any_spec),
        scratch_shapes=[
            vmem(full, f32),
            vmem(full, f32),
            vmem(full, net_load.dtype),
            vmem((site_count, horizon), f32),
            vmem(full, f32),
            vmem(full, f32),
            vmem(full, f32),
            vmem(full, f32),
            vmem(full, f32),
            vmem((3, site_count, horizon), f32),
            vmem((horizon, horizon), kern_type),
            vmem((6, scen_count, horizon), f32),
            vmem((5, site_count, horizon), f32),
            vmem((2, site_count, half), f32),
            vmem((2, site_count // 2, half), f32),
            vmem((n_scen - 1, site_count, half), f32),
            vmem((2, site_count // 2, half), f32),
            vmem((2, scen_count, horizon), f32),
            vmem((2, n_site - 1, scen_count, horizon), f32),
            vmem((scen_count, horizon), f32),
            dma((4, CHUNKS)),
            dma((CHUNKS + 1,)),
            dma((n_scen - 1,)),
            dma((n_scen - 1,)),
            dma((2,)),
            dma((2,)),
            dma((2, n_site - 1)),
            dma((2, n_site - 1)),
        ],
        compiler_params=pltpu.CompilerParams(
            collective_id=0, has_side_effects=True, vmem_limit_bytes=48 * 1024 * 1024
        ),
    )(
        dispatch,
        dual_price,
        net_load,
        energy_price,
        penalty,
        soc_weight,
        capacity,
        probability,
        node_deep,
    )


def solution(mesh):
    in_specs = (
        P(("group", "scen"), "site", None),
        P(("group", "scen"), "site", None),
        P(("group", "scen"), "site", None),
        P(("group", "site"), None),
        P("site"),
        P("site"),
        P("site"),
        P("group"),
        P("group"),
    )
    out_specs = (P(("group", "scen"), "site", None), P(("group", "scen"), "site", None))
    return jax.shard_map(
        functools.partial(body, mesh.shape["scen"], mesh.shape["site"]),
        mesh=mesh,
        in_specs=in_specs,
        out_specs=out_specs,
        check_vma=False,
    )
```

time: 79.6 us -> 24.5 us (0.31)
  blocking collectives: 42.7 us -> 0 us
  Pallas kernels: 0 us -> 14 us
  between operations: 14.2 us -> 0.66 us
  other arithmetic: 9.82 us -> 0 us
  matrix products: 7.24 us -> 0 us
  local copies, waits for them, and re-layouts: 5.17 us -> 9.54 us
    psum x3 -> x0, blocking collectives: 42.7 us -> none  [the longest x2 23.2 us: body(): imbalance = lax.psum(jnp.sum(current - load_float, axis=1), 'site')]
    pallas_call x0 -> x1, Pallas kernels: none -> 14 us  [body(): pl.pallas_call(functools.partial(kernel, n_scen, n_site), out_shape=(jax....]
    reduce_sum x4 -> x0, other arithmetic: 7.33 us -> none  [the longest x2 3.99 us: body(): imbalance = lax.psum(jnp.sum(current - load_float, axis=1), 'site')]
    dot_general x12 -> x0, matrix products: 7.24 us -> none  [the longest x2 2.62 us: body(): jnp.dot(charge_state, upper_ones.T, precision=precise)]
    unnamed x26 -> x20, local copies, waits for them, and re-layouts: 4.11 us -> 9.54 us
    min x1 -> x0, other arithmetic: 1.75 us -> none  [body(): current = jnp.clip(current - step_size * gradient, -limit, limit)]
    reshape x4 -> x0, local copies, waits for them, and re-layouts: 0.8 us -> none  [the longest x2 0.37 us: weighted_section(): return (my_prob[:, None, None] * piece).reshape(scen_count, width)]
  transfers between devices with their start and end apart: 1 -> 0, of which waited for: 0 -> 0; matrix products, arithmetic and copies ran while one was open for 7% -> 0% of each run, Pallas kernels for 0% -> 0%
where the time goes in v1:
time: 24.5 us; the launch traced here: 24.2 us
  Pallas kernels  14 us (57%)
  local copies, waits for them, and re-layouts  9.54 us (39%)
  between operations  0.66 us (3%)
    pallas_call x1, Pallas kernels, body(): pl.pallas_call(functools.partial(kernel, n_scen, n_site), out_shape=(jax....  14 us
    unnamed x20, local copies, waits for them, and re-layouts  9.54 us

profile of v1, /device:TPU:0, one launch (start us, length us, event | category | flops | bytes accessed | tf_op | source)
XLA Modules:
  0.0 24.2 jit_solution(3040994852204690545)
XLA Ops:
  0.6 0.0 copy-start
  0.6 1.2 %copy-done = f32[16,64,256]{2,1,0:T(8,128)S(1)} copy-done((f32[16,64,256]{2,1,0:T(8,128)S(1)}, f32[16,64,256]{2,1,0:T(8,128)}, u32[]{:S(2)}) %copy-start) | copy-done | bytes 1048600
  1.9 0.0 copy-start.1
  1.9 1.2 %copy-done.1 = f32[16,64,256]{2,1,0:T(8,128)S(1)} copy-done((f32[16,64,256]{2,1,0:T(8,128)S(1)}, f32[16,64,256]{2,1,0:T(8,128)}, u32[]{:S(2)}) %copy-start.1) | copy-done | bytes 1048600
  3.1 0.0 copy-start.2
  3.1 1.0 %copy-done.2 = bf16[16,64,256]{2,1,0:T(8,128)(2,1)S(1)} copy-done((bf16[16,64,256]{2,1,0:T(8,128)(2,1)S(1)}, bf16[16,64,256]{2,1,0:T(8,128)(2,1)}, u32[]{:S(2)}) %copy-start.2) | copy-done | bytes 524312
  4.1 0.0 copy-start.3
  4.1 0.8 %copy-done.3 = f32[64,256]{1,0:T(8,128)S(1)} copy-done((f32[64,256]{1,0:T(8,128)S(1)}, f32[64,256]{1,0:T(8,128)}, u32[]{:S(2)}) %copy-start.3) | copy-done | bytes 65560
  5.0 0.0 copy-start.4
  5.0 0.7 %copy-done.4 = f32[64]{0:T(128)S(1)} copy-done((f32[64]{0:T(128)S(1)}, f32[64]{0:T(128)}, u32[]{:S(2)}) %copy-start.4) | copy-done | bytes 280
  5.6 0.0 copy-start.5
  5.6 0.7 %copy-done.5 = f32[64]{0:T(128)S(1)} copy-done((f32[64]{0:T(128)S(1)}, f32[64]{0:T(128)}, u32[]{:S(2)}) %copy-start.5) | copy-done | bytes 280
  6.3 0.0 copy-start.6
  6.3 0.7 %copy-done.6 = f32[64]{0:T(128)S(1)} copy-done((f32[64]{0:T(128)S(1)}, f32[64]{0:T(128)}, u32[]{:S(2)}) %copy-start.6) | copy-done | bytes 280
  6.9 0.0 copy-start.7
  6.9 0.7 %copy-done.7 = f32[64]{0:T(128)S(1)} copy-done((f32[64]{0:T(128)S(1)}, f32[64]{0:T(128)}, u32[]{:S(2)}) %copy-start.7) | copy-done | bytes 280
  7.6 0.0 copy-start.8
  7.6 0.7 %copy-done.8 = s32[64]{0:T(128)S(1)} copy-done((s32[64]{0:T(128)S(1)}, s32[64]{0:T(128)}, u32[]{:S(2)}) %copy-start.8) | copy-done | bytes 280
  8.2 14.0 %shard_map.104 = (f32[16,64,256]{2,1,0:T(8,128)S(1)}, f32[16,64,256]{2,1,0:T(8,128)S(1)}) custom-call(f32[16,64,256]{2,1,0:T(8,128)S(1)} %copy-done, f32[16,64,256]{2,1,0:T(8,128)S(1)} %copy-done.1, bf16[16,64,256]{2,1,0:T(8,128)(2,1)S(1)} %copy-done.2, f32[64,256]{1,0:T(8,128)S(1)} %copy-done.3, f32[64]{0:T(128)S(1)} %copy-done.4, f32[64]{0:T(128)S(1)} %copy-done.5, ...), custom_call_target="tpu_custom_call" | custom-call | tf_op jit(solution)/shard_map/pallas_call | solution.py:420
  22.2 1.0 %copy.13 = f32[16,64,256]{2,1,0:T(8,128)} copy(f32[16,64,256]{2,1,0:T(8,128)S(1)} %get-tuple-element.4) | data formatting | bytes 2097152
  23.2 1.0 %copy.14 = f32[16,64,256]{2,1,0:T(8,128)} copy(f32[16,64,256]{2,1,0:T(8,128)S(1)} %get-tuple-element.5) | data formatting | bytes 2097152
Async XLA Ops:
  0.6 1.2 %copy-start = (f32[16,64,256]{2,1,0:T(8,128)S(1)}, f32[16,64,256]{2,1,0:T(8,128)}, u32[]{:S(2)}) copy-start(f32[16,64,256]{2,1,0:T(8,128)} %disp_hbm.1) | copy-start | bytes 3145732
  1.9 1.2 %copy-start.1 = (f32[16,64,256]{2,1,0:T(8,128)S(1)}, f32[16,64,256]{2,1,0:T(8,128)}, u32[]{:S(2)}) copy-start(f32[16,64,256]{2,1,0:T(8,128)} %dual_hbm.1) | copy-start | bytes 3145732
  3.1 1.0 %copy-start.2 = (bf16[16,64,256]{2,1,0:T(8,128)(2,1)S(1)}, bf16[16,64,256]{2,1,0:T(8,128)(2,1)}, u32[]{:S(2)}) copy-start(bf16[16,64,256]{2,1,0:T(8,128)(2,1)} %load_hbm.1) | copy-start | bytes 1572868
  4.1 0.8 %copy-start.3 = (f32[64,256]{1,0:T(8,128)S(1)}, f32[64,256]{1,0:T(8,128)}, u32[]{:S(2)}) copy-start(f32[64,256]{1,0:T(8,128)} %energy_hbm.1) | copy-start | bytes 196612
  5.0 0.7 %copy-start.4 = (f32[64]{0:T(128)S(1)}, f32[64]{0:T(128)}, u32[]{:S(2)}) copy-start(f32[64]{0:T(128)} %pen_ref.1) | copy-start | bytes 772
  5.6 0.7 %copy-start.5 = (f32[64]{0:T(128)S(1)}, f32[64]{0:T(128)}, u32[]{:S(2)}) copy-start(f32[64]{0:T(128)} %soc_ref.1) | copy-start | bytes 772
  6.3 0.7 %copy-start.6 = (f32[64]{0:T(128)S(1)}, f32[64]{0:T(128)}, u32[]{:S(2)}) copy-start(f32[64]{0:T(128)} %cap_ref.1) | copy-start | bytes 772
  6.9 0.7 %copy-start.7 = (f32[64]{0:T(128)S(1)}, f32[64]{0:T(128)}, u32[]{:S(2)}) copy-start(f32[64]{0:T(128)} %prob_ref.1) | copy-start | bytes 772
  7.6 0.7 %copy-start.8 = (s32[64]{0:T(128)S(1)}, s32[64]{0:T(128)}, u32[]{:S(2)}) copy-start(s32[64]{0:T(128)} %node_ref.1) | copy-start | bytes 772

commit v2 on v1

--- a/solution.py
+++ b/solution.py
@@ -19,22 +19,27 @@
     dual_hbm,
     load_hbm,
     energy_hbm,
+    pen_hbm,
+    soc_hbm,
+    cap_hbm,
+    prob_hbm,
+    node_hbm,
+    z_ref,
+    nd_ref,
+    imb_out,
+    col_out,
     pen_ref,
     soc_ref,
     cap_ref,
     prob_ref,
     node_ref,
-    out_hbm,
-    ndual_hbm,
     x_ref,
     dual_ref,
     load_ref,
     energy_ref,
     floc_ref,
     q_ref,
-    z_ref,
     cur_ref,
-    nd_ref,
     fin_ref,
     kern_ref,
     tab_ref,
@@ -47,7 +52,7 @@
     imbr_ref,
     loadsum_ref,
     in_sem,
-    out_sem,
+    small_sem,
     scen_send,
     scen_recv,
     deep_send,
@@ -68,6 +73,20 @@
     def fetch(c, which, src, dst):
         return pltpu.make_async_copy(src.at[rows(c)], dst.at[rows(c)], in_sem.at[which, c])
 
+    smalls = [
+        pltpu.make_async_copy(src, dst, small_sem.at[i])
+        for i, (src, dst) in enumerate(
+            (
+                (prob_hbm, prob_ref),
+                (node_hbm, node_ref),
+                (pen_hbm, pen_ref),
+                (soc_hbm, soc_ref),
+                (cap_hbm, cap_ref),
+            )
+        )
+    ]
+    for copy in smalls:
+        copy.start()
     ins = []
     for c in range(CHUNKS):
         ins.append((fetch(c, 0, disp_hbm, x_ref), fetch(c, 1, load_hbm, load_ref)))
@@ -96,6 +115,9 @@
         pl.semaphore_signal(
             barrier, inc=1, device_id={"site": lax.rem(here + j, n_site)}, device_id_type=MESH
         )
+
+    for copy in smalls:
+        copy.wait()
 
     total = prob_ref.shape[0]
     first_row = me * scen_count
@@ -159,8 +181,8 @@
     col_ref[0] = jnp.broadcast_to(pen, wide)
     col_ref[1] = jnp.broadcast_to(step, wide)
     col_ref[2] = jnp.broadcast_to(step * column(soc_ref) / (horizon * horizon), wide)
-    col_ref[3] = jnp.broadcast_to(step * (2.0 / sites_all), wide)
-    col_ref[4] = jnp.broadcast_to(column(cap_ref), wide)
+    col_out[0] = jnp.broadcast_to(step * (2.0 / sites_all), wide)
+    col_out[1] = jnp.broadcast_to(column(cap_ref), wide)
     hour_a = lax.broadcasted_iota(jnp.int32, (horizon, horizon), 0)
     hour_b = lax.broadcasted_iota(jnp.int32, (horizon, horizon), 1)
     kern_ref[...] = (horizon - jnp.maximum(hour_a, hour_b)).astype(jnp.float32).astype(kern_ref.dtype)
@@ -337,8 +359,8 @@
             - row(tab_ref.at[5], s) * fin_ref[2]
         )
         nd_ref[s] = dual_ref[s] + q
-        cap = col_ref[4]
-        new = z_ref[s] - 2.0 * col_ref[1] * q - col_ref[3] * row(tab_ref.at[0], s)
+        cap = col_out[1]
+        new = z_ref[s] - 2.0 * col_ref[1] * q - col_out[0] * row(tab_ref.at[0], s)
         new = jnp.minimum(jnp.maximum(new, -cap), cap)
         cur_ref[s] = new
         imb_ref[1, pl.ds(s, 1), :] = jnp.sum(new, axis=0, keepdims=True) - row(loadsum_ref, s)
@@ -346,8 +368,6 @@
     sites_second = site_copies(1)
     for copy in sites_second:
         copy.start()
-    dual_out = pltpu.make_async_copy(nd_ref, ndual_hbm, out_sem.at[0])
-    dual_out.start()
 
     for c in range(CHUNKS):
         ahead = ahead_of(cur_ref, c)
@@ -367,30 +387,34 @@
     imb_two = imb_ref[1]
     for j in range(n_site - 1):
         imb_two = imb_two + imbr_ref[1, j]
-    tab_ref[1] = imb_two
-    outs = []
+    imb_out[...] = imb_two
+
+    for copy in scen_copies + sites_first + sites_second:
+        copy.wait_send()
+
+    @pl.when(has_right)
+    def _():
+        deep_copies[0].wait_send()
+
+    @pl.when(has_left)
+    def _():
+        deep_copies[1].wait_send()
+
+
+def finish(z_ref, nd_ref, imb_ref, col_ref, out_hbm, ndual_hbm, new_ref, out_sem):
+    scen_count = z_ref.shape[0]
+    step_rows = scen_count // CHUNKS
+    outs = [pltpu.make_async_copy(nd_ref, ndual_hbm, out_sem.at[CHUNKS])]
+    outs[0].start()
+    cap = col_ref[1]
     for c in range(CHUNKS):
-        for i in range(step_rows):
-            s = c * step_rows + i
-            cap = col_ref[4]
-            new = z_ref[s] - col_ref[3] * row(tab_ref.at[1], s)
-            q_ref[s] = jnp.minimum(jnp.maximum(new, -cap), cap)
-        copy = pltpu.make_async_copy(q_ref.at[rows(c)], out_hbm.at[rows(c)], out_sem.at[c + 1])
+        for s in range(c * step_rows, (c + 1) * step_rows):
+            new = z_ref[s] - col_ref[0] * imb_ref[pl.ds(s, 1), :]
+            new_ref[s] = jnp.minimum(jnp.maximum(new, -cap), cap)
+        part = pl.ds(c * step_rows, step_rows)
+        copy = pltpu.make_async_copy(new_ref.at[part], out_hbm.at[part], out_sem.at[c])
         copy.start()
         outs.append(copy)
-
-    for copy in scen_copies + sites_first + sites_second:
-        copy.wait_send()
-
-    @pl.when(has_right)
-    def _():
-        deep_copies[0].wait_send()
-
-    @pl.when(has_left)
-    def _():
-        deep_copies[1].wait_send()
-
-    dual_out.wait()
     for copy in outs:
         copy.wait()
 
@@ -413,16 +437,31 @@
     full = (scen_count, site_count, horizon)
     half = horizon // 2
     vmem = pltpu.VMEM
-    any_spec = pl.BlockSpec(memory_space=pl.ANY)
+    hbm_spec = pl.BlockSpec(memory_space=pltpu.HBM)
     vmem_spec = pl.BlockSpec(memory_space=vmem)
     kern_type = jnp.bfloat16 if horizon <= 256 else f32
     dma = pltpu.SemaphoreType.DMA
-    return pl.pallas_call(
+    shape = jax.ShapeDtypeStruct
+    big = [
+        pltpu.with_memory_space_constraint(x, pltpu.HBM)
+        for x in (dispatch, dual_price, net_load, energy_price, penalty, soc_weight, capacity, probability, node_deep)
+    ]
+    parts = pl.pallas_call(
         functools.partial(kernel, n_scen, n_site),
-        out_shape=(jax.ShapeDtypeStruct(full, f32), jax.ShapeDtypeStruct(full, f32)),
-        in_specs=[any_spec] * 4 + [vmem_spec] * 5,
-        out_specs=(any_spec, any_spec),
+        out_shape=(
+            shape(full, f32),
+            shape(full, f32),
+            shape((scen_count, horizon), f32),
+            shape((2, site_count, horizon), f32),
+        ),
+        in_specs=[hbm_spec] * 9,
+        out_specs=(vmem_spec,) * 4,
         scratch_shapes=[
+            vmem(penalty.shape, f32),
+            vmem(penalty.shape, f32),
+            vmem(penalty.shape, f32),
+            vmem(probability.shape, f32),
+            vmem(node_deep.shape, node_deep.dtype),
             vmem(full, f32),
             vmem(full, f32),
             vmem(full, net_load.dtype),
@@ -430,12 +469,10 @@
             vmem(full, f32),
             vmem(full, f32),
             vmem(full, f32),
-            vmem(full, f32),
-            vmem(full, f32),
             vmem((3, site_count, horizon), f32),
             vmem((horizon, horizon), kern_type),
             vmem((6, scen_count, horizon), f32),
-            vmem((5, site_count, horizon), f32),
+            vmem((3, site_count, horizon), f32),
             vmem((2, site_count, half), f32),
             vmem((2, site_count // 2, half), f32),
             vmem((n_scen - 1, site_count, half), f32),
@@ -444,7 +481,7 @@
             vmem((2, n_site - 1, scen_count, horizon), f32),
             vmem((scen_count, horizon), f32),
             dma((4, CHUNKS)),
-            dma((CHUNKS + 1,)),
+            dma((5,)),
             dma((n_scen - 1,)),
             dma((n_scen - 1,)),
             dma((2,)),
@@ -453,19 +490,17 @@
             dma((2, n_site - 1)),
         ],
         compiler_params=pltpu.CompilerParams(
-            collective_id=0, has_side_effects=True, vmem_limit_bytes=48 * 1024 * 1024
+            collective_id=0, has_side_effects=True, vmem_limit_bytes=24 * 1024 * 1024
         ),
-    )(
-        dispatch,
-        dual_price,
-        net_load,
-        energy_price,
-        penalty,
-        soc_weight,
-        capacity,
-        probability,
-        node_deep,
-    )
+    )(*big)
+    return pl.pallas_call(
+        finish,
+        out_shape=(shape(full, f32), shape(full, f32)),
+        in_specs=[vmem_spec] * 4,
+        out_specs=(hbm_spec, hbm_spec),
+        scratch_shapes=[vmem(full, f32), dma((CHUNKS + 1,))],
+        compiler_params=pltpu.CompilerParams(vmem_limit_bytes=24 * 1024 * 1024),
+    )(*parts)
 
 
 def solution(mesh):

time: 24.5 us -> 15.7 us (0.64)
  local copies, waits for them, and re-layouts: 9.54 us -> 0 us
  Pallas kernels: 14 us -> 14.9 us
    unnamed x20 -> x0, local copies, waits for them, and re-layouts: 9.54 us -> none
    pallas_call x1 -> x2, Pallas kernels: 14 us -> 14.9 us  [the longest x1 13.5 us: body(): pl.pallas_call(functools.partial(kernel, n_scen, n_site), out_shape=(shap...]
where the time goes in v2:
time: 15.7 us; the launch traced here: 15.5 us
  Pallas kernels  14.9 us (95%)
  between operations  0.64 us (4%)
    pallas_call x1, Pallas kernels, body(): pl.pallas_call(functools.partial(kernel, n_scen, n_site), out_shape=(shap...  13.5 us
    pallas_call x1, Pallas kernels, body(): pl.pallas_call(finish, out_shape=(shape(full, f32), shape(full, f32)), in...  1.35 us

profile of v2, /device:TPU:0, one launch (start us, length us, event | category | flops | bytes accessed | tf_op | source)
XLA Modules:
  0.0 15.5 jit_solution(13067722250330753019)
XLA Ops:
  0.6 13.5 %shard_map.104 = (f32[16,64,256]{2,1,0:T(8,128)S(1)}, f32[16,64,256]{2,1,0:T(8,128)S(1)}, f32[16,256]{1,0:T(8,128)S(1)}, f32[2,64,256]{2,1,0:T(8,128)S(1)}) custom-call(f32[16,64,256]{2,1,0:T(8,128)} %disp_hbm.1, f32[16,64,256]{2,1,0:T(8,128)} %dual_hbm.1, bf16[16,64,256]{2,1,0:T(8,128)(2,1)} %load_hbm.1, f32[64,256]{1,0:T(8,128)} %energy_hbm.1, f32[64]{0:T(128)} %pen_hbm.1, ...), custom_call_target="tpu_custom_call" | custom-call | tf_op jit(solution)/shard_map/pallas_call | solution.py:449
  14.2 1.4 %shard_map.105 = (f32[16,64,256]{2,1,0:T(8,128)}, f32[16,64,256]{2,1,0:T(8,128)}) custom-call(f32[16,64,256]{2,1,0:T(8,128)S(1)} %get-tuple-element.6.z_ref, f32[16,64,256]{2,1,0:T(8,128)S(1)} %get-tuple-element.7.nd_ref, f32[16,256]{1,0:T(8,128)S(1)} %get-tuple-element.8.imb_ref, f32[2,64,256]{2,1,0:T(8,128)S(1)} %get-tuple-element.9.col_ref), custom_call_target="tpu_custom_call" | custom-call | tf_op jit(solution)/shard_map/pallas_call | solution.py:496

commit v3 on v2

--- a/solution.py
+++ b/solution.py
@@ -73,6 +73,17 @@
     def fetch(c, which, src, dst):
         return pltpu.make_async_copy(src.at[rows(c)], dst.at[rows(c)], in_sem.at[which, c])
 
+    barrier = pltpu.get_barrier_semaphore()
+    for j in range(1, n_scen):
+        pl.semaphore_signal(
+            barrier, inc=1, device_id={"scen": lax.rem(me + j, n_scen)}, device_id_type=MESH
+        )
+    for j in range(1, n_site):
+        pl.semaphore_signal(
+            barrier, inc=1, device_id={"site": lax.rem(here + j, n_site)}, device_id_type=MESH
+        )
+
+
     smalls = [
         pltpu.make_async_copy(src, dst, small_sem.at[i])
         for i, (src, dst) in enumerate(
@@ -91,6 +102,7 @@
     for c in range(CHUNKS):
         ins.append((fetch(c, 0, disp_hbm, x_ref), fetch(c, 1, load_hbm, load_ref)))
         ins[c][0].start()
+    for c in range(CHUNKS):
         ins[c][1].start()
     energy_in = pltpu.make_async_copy(energy_hbm, energy_ref, in_sem.at[3, 0])
     energy_in.start()
@@ -105,16 +117,6 @@
     @pl.when(me == n_scen - 1)
     def _():
         gotd_ref[1] = jnp.zeros_like(gotd_ref[1])
-
-    barrier = pltpu.get_barrier_semaphore()
-    for j in range(1, n_scen):
-        pl.semaphore_signal(
-            barrier, inc=1, device_id={"scen": lax.rem(me + j, n_scen)}, device_id_type=MESH
-        )
-    for j in range(1, n_site):
-        pl.semaphore_signal(
-            barrier, inc=1, device_id={"site": lax.rem(here + j, n_site)}, device_id_type=MESH
-        )
 
     for copy in smalls:
         copy.wait()
@@ -206,12 +208,8 @@
     first_sum = None
     for c in range(CHUNKS):
         ins[c][0].wait()
-        ins[c][1].wait()
         for s in range(c * step_rows, (c + 1) * step_rows):
             x = x_ref[s]
-            load_total = jnp.sum(load_ref[s].astype(jnp.float32), axis=0, keepdims=True)
-            loadsum_ref[pl.ds(s, 1), :] = load_total
-            imb_ref[0, pl.ds(s, 1), :] = jnp.sum(x, axis=0, keepdims=True) - load_total
             weighted = x * row(tab_ref.at[0], s)
             fore = weighted if fore is None else weighted + row(tab_ref.at[1], s) * fore
             floc_ref[s] = fore
@@ -263,13 +261,13 @@
     has_right = me < n_scen - 1
     has_left = me > 0
 
-    def site_copies(turn):
+    def site_copies(turn, lanes, index):
         return [
             pltpu.make_async_remote_copy(
-                src_ref=imb_ref.at[turn],
-                dst_ref=imbr_ref.at[turn, j - 1],
-                send_sem=site_send.at[turn, j - 1],
-                recv_sem=site_recv.at[turn, j - 1],
+                src_ref=imb_ref.at[turn, :, lanes],
+                dst_ref=imbr_ref.at[turn, j - 1, :, lanes],
+                send_sem=site_send.at[index, j - 1],
+                recv_sem=site_recv.at[index, j - 1],
                 device_id={"site": lax.rem(here + j, n_site)},
                 device_id_type=MESH,
             )
@@ -287,7 +285,14 @@
     def _():
         deep_copies[1].start()
 
-    sites_first = site_copies(0)
+
+    for c in range(CHUNKS):
+        ins[c][1].wait()
+        for s in range(c * step_rows, (c + 1) * step_rows):
+            load_total = jnp.sum(load_ref[s].astype(jnp.float32), axis=0, keepdims=True)
+            loadsum_ref[pl.ds(s, 1), :] = load_total
+            imb_ref[0, pl.ds(s, 1), :] = jnp.sum(x_ref[s], axis=0, keepdims=True) - load_total
+    sites_first = site_copies(0, pl.ds(0, horizon), 0)
     for copy in sites_first:
         copy.start()
 
@@ -336,6 +341,27 @@
         imb_one = imb_one + imbr_ref[0, j]
     tab_ref[0] = imb_one
 
+    def update(lanes):
+        for s in range(scen_count):
+            spot = pl.ds(s, 1)
+            q = (
+                q_ref[s, :, lanes]
+                - tab_ref[4, spot, lanes] * fin_ref[1, :, lanes]
+                - tab_ref[5, spot, lanes] * fin_ref[2, :, lanes]
+            )
+            nd_ref[s, :, lanes] = dual_ref[s, :, lanes] + q
+            cap = col_out[1, :, lanes]
+            new = (
+                z_ref[s, :, lanes]
+                - 2.0 * col_ref[1, :, lanes] * q
+                - col_out[0, :, lanes] * tab_ref[0, spot, lanes]
+            )
+            new = jnp.minimum(jnp.maximum(new, -cap), cap)
+            cur_ref[s, :, lanes] = new
+            imb_ref[1, spot, lanes] = (
+                jnp.sum(new, axis=0, keepdims=True) - loadsum_ref[spot, lanes]
+            )
+
     @pl.when(has_left)
     def _():
         deep_copies[0].wait_recv()
@@ -343,31 +369,27 @@
     @pl.when(has_right)
     def _():
         deep_copies[1].wait_recv()
+
+    late, early = pl.ds(half, half), pl.ds(0, half)
+    fin_ref[1, :, late] = col_ref[0, :, late] * (gate_left * unpack(gotd_ref[0]))
+    fin_ref[2, :, late] = col_ref[0, :, late] * (gate_right * unpack(gotd_ref[1]))
+    update(late)
+    sites_late = site_copies(1, late, 1)
+    for copy in sites_late:
+        copy.start()
 
     for j in range(1, n_scen):
         scen_copies[j - 1].wait_recv()
         got = got_ref[j - 1]
         left = left + gates[j - 1][0] * got
         right = right + gates[j - 1][1] * got
-    fin_ref[1] = col_ref[0] * jnp.concatenate([left, gate_left * unpack(gotd_ref[0])], axis=1)
-    fin_ref[2] = col_ref[0] * jnp.concatenate([right, gate_right * unpack(gotd_ref[1])], axis=1)
-
-    for s in range(scen_count):
-        q = (
-            q_ref[s]
-            - row(tab_ref.at[4], s) * fin_ref[1]
-            - row(tab_ref.at[5], s) * fin_ref[2]
-        )
-        nd_ref[s] = dual_ref[s] + q
-        cap = col_out[1]
-        new = z_ref[s] - 2.0 * col_ref[1] * q - col_out[0] * row(tab_ref.at[0], s)
-        new = jnp.minimum(jnp.maximum(new, -cap), cap)
-        cur_ref[s] = new
-        imb_ref[1, pl.ds(s, 1), :] = jnp.sum(new, axis=0, keepdims=True) - row(loadsum_ref, s)
-
-    sites_second = site_copies(1)
-    for copy in sites_second:
+    fin_ref[1, :, early] = col_ref[0, :, early] * left
+    fin_ref[2, :, early] = col_ref[0, :, early] * right
+    update(early)
+    sites_early = site_copies(1, early, 2)
+    for copy in sites_early:
         copy.start()
+    sites_second = sites_late + sites_early
 
     for c in range(CHUNKS):
         ahead = ahead_of(cur_ref, c)
@@ -486,8 +508,8 @@
             dma((n_scen - 1,)),
             dma((2,)),
             dma((2,)),
-            dma((2, n_site - 1)),
-            dma((2, n_site - 1)),
+            dma((3, n_site - 1)),
+            dma((3, n_site - 1)),
         ],
         compiler_params=pltpu.CompilerParams(
             collective_id=0, has_side_effects=True, vmem_limit_bytes=24 * 1024 * 1024

time: 15.7 us -> 15.2 us (0.968)
  Pallas kernels: 14.9 us -> 14.4 us
    pallas_call x1, Pallas kernels: 13.5 us -> 13.1 us  [body(): pl.pallas_call(functools.partial(kernel, n_scen, n_site), out_shape=(shap...]
where the time goes in v3:
time: 15.2 us; the launch traced here: 15.1 us
  Pallas kernels  14.4 us (95%)
  between operations  0.64 us (4%)
    pallas_call x1, Pallas kernels, body(): pl.pallas_call(functools.partial(kernel, n_scen, n_site), out_shape=(shap...  13.1 us
    pallas_call x1, Pallas kernels, body(): pl.pallas_call(finish, out_shape=(shape(full, f32), shape(full, f32)), in...  1.35 us

profile of v3, /device:TPU:0, one launch (start us, length us, event | category | flops | bytes accessed | tf_op | source)
XLA Modules:
  0.0 15.1 jit_solution(18041712421416082846)
XLA Ops:
  0.6 13.1 %shard_map.104 = (f32[16,64,256]{2,1,0:T(8,128)S(1)}, f32[16,64,256]{2,1,0:T(8,128)S(1)}, f32[16,256]{1,0:T(8,128)S(1)}, f32[2,64,256]{2,1,0:T(8,128)S(1)}) custom-call(f32[16,64,256]{2,1,0:T(8,128)} %disp_hbm.1, f32[16,64,256]{2,1,0:T(8,128)} %dual_hbm.1, bf16[16,64,256]{2,1,0:T(8,128)(2,1)} %load_hbm.1, f32[64,256]{1,0:T(8,128)} %energy_hbm.1, f32[64]{0:T(128)} %pen_hbm.1, ...), custom_call_target="tpu_custom_call" | custom-call | tf_op jit(solution)/shard_map/pallas_call | solution.py:471
  13.7 1.4 %shard_map.105 = (f32[16,64,256]{2,1,0:T(8,128)}, f32[16,64,256]{2,1,0:T(8,128)}) custom-call(f32[16,64,256]{2,1,0:T(8,128)S(1)} %get-tuple-element.6.z_ref, f32[16,64,256]{2,1,0:T(8,128)S(1)} %get-tuple-element.7.nd_ref, f32[16,256]{1,0:T(8,128)S(1)} %get-tuple-element.8.imb_ref, f32[2,64,256]{2,1,0:T(8,128)S(1)} %get-tuple-element.9.col_ref), custom_call_target="tpu_custom_call" | custom-call | tf_op jit(solution)/shard_map/pallas_call | solution.py:518
